TPU v7x, 512 devices: a whole 4x8x8 slice. The times are simulated.
512 devices in a mesh: depth: 8 (over y), lat: 32 (over z, x), freq: 2 (over core).
Axes of the slice: x: 4, y: 8, z: 8, core: 2. Of those that a mesh axis runs over, the one named last changes fastest.
Arguments:
- surface: bfloat16 [6, 2, 128, 32768], P('freq', None, None, 'lat'), may hold values from -6 to 6
- refl: float32 [8, 32768], P('depth', 'lat'), may hold values from -0.5 to 0.5
- pool: bfloat16 [8, 6, 8, 128, 256], P('depth', 'freq'), may hold values from -0.375 to 0.375
- tile_ids: int32 [8, 256, 10], P('depth', 'lat'), may hold values from 0 to 255, as said below
- block_ids: int32 [8, 256, 10], P('depth', 'lat'), may hold values from 0 to 7
- counts: int32 [8, 256], P('depth', 'lat'), may hold values from 1 to 10, as said below
Outputs:
- image: float32 [8, 32768], P('depth', 'lat')
Inputs may be any that keep to these rules, and one draw needn't show every extreme that they name: tile_ids[l, j, k] = (j + o) mod 256 for an offset o with -8 <= o <= 8; slot 0 names the row's own tile; in every level some row has all 10 slots live with offsets 8 at slot 1 and -8 at slot 2. Slots k >= counts[l, j] of row j are padding; in every level some row has all 10 slots live.
All inputs are finite; a program needn't handle non-finite values.
Results may differ from a plain program's by a relative error of at most 0.00055.
Values may be sent and summed in bfloat16 or wider, within the bound.
A program may use at most 128 MiB of HBM per device.

v0:
```python
import jax
import jax.numpy as jnp
from jax import lax
from jax.sharding import PartitionSpec as P

TILE = 128
TILE_DEV = 8


def extended_2(block, sides, width):
    for axis, dim in sides:
        count = lax.axis_size(axis)
        forward = [(i, i + 1) for i in range(count - 1)]
        forward.append((count - 1, 0))
        backward = [(target, source) for source, target in forward]
        low = lax.ppermute(
            lax.slice_in_dim(block, block.shape[dim] - width, None, axis=dim), axis, forward
        )
        high = lax.ppermute(lax.slice_in_dim(block, 0, width, axis=dim), axis, backward)
        block = jnp.concatenate([low, block, high], axis=dim)
    return block


def in_one_piece(arrays, axis, dim, along):
    columns = [a.reshape(*a.shape[:along], -1) for a in arrays]
    both = jnp.concatenate(columns, axis=along)
    whole, at, gathered = (lax.all_gather(both, axis, axis=dim, tiled=True), 0, [])
    for a, column in zip(arrays, columns):
        piece = whole[..., at : at + column.shape[along]]
        gathered.append(piece.reshape(*piece.shape[:along], *a.shape[along:]))
        at += column.shape[along]
    return tuple(gathered)


def copy_for_each(shard, axis):
    copies = jnp.broadcast_to(shard, (lax.axis_size(axis), *shard.shape))
    return lax.all_to_all(copies, axis, split_axis=0, concat_axis=0, tiled=True)


def in_order(parts, dim):
    parts = jnp.moveaxis(parts, 0, dim)
    shape = parts.shape
    return parts.reshape(*shape[:dim], shape[dim] * shape[dim + 1], *shape[dim + 2 :])


def gather_directly(shard, axis, dim):
    parts = copy_for_each(shard, axis)
    return in_order(parts, dim)


def cut_along(shard, dim, length):
    before, after = (shard.shape[:dim], shard.shape[dim + 1 :])
    return jnp.moveaxis(shard.reshape(*before, length, -1, *after), dim, 0)


def summed_on_arrival(shard, axis, dim):
    parts = cut_along(shard, dim, lax.axis_size(axis))
    arrived = lax.all_to_all(parts, axis, split_axis=0, concat_axis=0, tiled=True)
    return arrived.sum(axis=0)


def aperture_rim(wave_field):
    return extended_2(wave_field, (("lat", 3),), TILE_DEV * TILE)


def extrapolate(extended, pool_level, local_ids, block_level, count_level, refl_level):
    freqs_here = extended.shape[0]
    shot_rows = extended.shape[2]
    tile_rows = local_ids.shape[0]
    slot_total = local_ids.shape[1]
    tile_grid = extended.reshape(freqs_here, 2, shot_rows, -1, TILE)
    slot_live = (jnp.arange(slot_total)[None, :] < count_level[:, None]).astype(jnp.bfloat16)
    picked = jnp.take(tile_grid, local_ids, axis=3) * slot_live[None, None, None, :, :, None]
    chosen = jnp.take(pool_level, block_level, axis=1)
    product = jnp.einsum("fsarkt,frktc->rfsac", picked, chosen, preferred_element_type=jnp.float32)
    real_part = product[:, :, 0, :, :TILE] - product[:, :, 1, :, TILE:]
    imag_part = product[:, :, 0, :, TILE:] + product[:, :, 1, :, :TILE]
    row_scale = 1.0 / jnp.sqrt(count_level.astype(jnp.float32))
    rows_out = jnp.stack([real_part, imag_part], 2) * row_scale[:, None, None, None, None]
    wave_out = jnp.transpose(rows_out, (1, 2, 3, 0, 4)).reshape(
        freqs_here, 2, shot_rows, tile_rows * TILE
    )
    wave_out = wave_out * (1.0 - refl_level)
    return (wave_out.astype(jnp.bfloat16), jnp.sum(wave_out * wave_out, axis=(0, 1, 2)))


def per_device(surface, refl, pool, tile_ids, block_ids, counts):
    depth_index = lax.axis_index("depth")
    lat_index = lax.axis_index("lat")
    tile_count = TILE_DEV * lax.axis_size("lat")
    first_tile = lat_index * TILE_DEV - TILE_DEV
    freqs_here = surface.shape[0]
    shot_total = surface.shape[2]
    lateral_width = surface.shape[3]
    shot_rows = shot_total // lax.axis_size("depth")
    own_shots = lax.dynamic_slice_in_dim(surface, depth_index * shot_rows, shot_rows, 2)
    pool_all = lax.all_gather(pool, "depth", axis=0, tiled=True)
    ids_all, blocks_all, counts_all = in_one_piece((tile_ids, block_ids, counts), "depth", 0, 2)
    refl_all = gather_directly(refl, "depth", 0)
    level_total = pool_all.shape[0]

    def level_step(level_index, loop_state):
        wave_field, images = loop_state
        ids_here = lax.dynamic_index_in_dim(ids_all, level_index, 0, keepdims=False)
        local_level = jnp.mod(ids_here - first_tile, tile_count)
        pool_here = lax.dynamic_index_in_dim(pool_all, level_index, 0, keepdims=False)
        blocks_here = lax.dynamic_index_in_dim(blocks_all, level_index, 0, keepdims=False)
        counts_here = lax.dynamic_index_in_dim(counts_all, level_index, 0, keepdims=False)
        refl_here = lax.dynamic_index_in_dim(refl_all, level_index, 0, keepdims=False)
        handed, partial_value = extrapolate(
            aperture_rim(wave_field), pool_here, local_level, blocks_here, counts_here, refl_here
        )
        images = lax.dynamic_update_index_in_dim(images, partial_value, level_index, 0)
        return (handed, images)

    start_images = jnp.zeros((level_total, lateral_width), jnp.float32)
    loop_state = lax.fori_loop(0, level_total, level_step, (own_shots, start_images))
    image_local = summed_on_arrival(loop_state[1], "depth", 0)[0]
    summed = lax.psum(image_local, "freq")
    divisor = freqs_here * lax.axis_size("freq") * shot_total
    return (summed / divisor)[None, :]


def solution(mesh):
    placed = (
        P("freq", None, None, "lat"),
        P("depth", "lat"),
        P("depth", "freq", None, None, None),
        P("depth", "lat", None),
        P("depth", "lat", None),
        P("depth", "lat"),
    )
    return jax.shard_map(
        per_device, mesh=mesh, in_specs=placed, out_specs=P("depth", "lat"), check_vma=False
    )
```

profile of v0, /device:TPU:1, one launch (start us, length us, event | category | flops | bytes accessed | tf_op | source)
XLA Modules:
  0.0 460.4 jit_solution(3497054629939524282)
XLA Ops:
  8.6 7.7 %all-to-all-start = ((f32[8,1,1024]{2,1,0:T(1,128)}), f32[8,1,1024]{2,1,0:T(1,128)S(1)}, u32[]{:S(2)}, u32[]{:S(2)}) async-start(f32[8,1,1024]{2,1,0:T(1,128)} %broadcast_in_dim.88), calls=%async_computation | async-start | bytes 65536 | tf_op jit(solution)/shard_map/all_to_all | solution.py:37
  17.7 20.8 %all_gather.6 = s32[8,8,21]{2,1,0:T(8,128)S(1)} all-gather(s32[1,8,21]{2,1,0:T(8,128)S(1)} %pad_add_fusion), channel_id=1, replica_groups=mesh['depth'=8,'lat'=32,'freq'=2] {'depth'}, dimensions={0}, use_global_device_ids=true | all-gather | bytes 6048 | tf_op jit(solution)/shard_map/all_gather | solution.py:27
  40.0 110.9 %all-gather.2.cloned.1.call-done = bf16[8,3,8,128,256]{4,3,2,1,0:T(8,128)(2,1)} async-done(((bf16[1,3,8,128,256]{4,3,2,1,0:T(8,128)(2,1)}), bf16[8,3,8,128,256]{4,3,2,1,0:T(8,128)(2,1)}) %all-gather.2.cloned.1.call-update) | async-done | bytes 12582928 | tf_op jit(solution)/shard_map/all_gather | solution.py:97
  150.9 281.9 %while.17 = (s32[]{:T(128)}, bf16[3,2,16,1024]{3,2,1,0:T(8,128)(2,1)S(1)}, f32[8,1024]{1,0:T(8,128)}, s32[8,8,10]{2,1,0:T(8,128)S(1)}, s32[]{:T(128)}, /*index=5...) while((s32[]{:T(128)}, ...), condition=%wide.region_2.3_spmd, body=%wide.region_0.2_spmd.sunk | while | flops 515904960 | bytes 62015692 | solution.py:117
  150.9 7.8 %collective-permute-start = (bf16[3,2,16,1024]{3,2,1,0:T(8,128)(2,1)S(1)}, bf16[3,2,16,1024]{3,2,1,0:T(8,128)(2,1)S(1)}, u32[]{:S(2)}, u32[]{:S(2)}) collective-permute-start(bf16[3,2,16,1024]{3,2,1,0:T(8,128)(2,1)S(1)} %get-tuple-element.365), channel_id=1, source_target_pairs={{2,0},{4,2},{6,4},{8,6},{10,8},{12,10},{14,12},{16,14},{18,16},{20... | collective-permute-start | bytes 589832 | tf_op jit(solution)/shard_map/while/body/eval_jaxpr/ppermute | solution.py:19
  164.9 8.1 %gather_fusion = bf16[80,3,128,256]{3,2,1,0:T(8,128)(2,1)} fusion(bf16[3,8,128,256]{3,2,1,0:T(8,128)(2,1)S(1)} %dynamic-slice_bitcast_fusion.2, s32[1024]{0:T(1024)S(1)} %pad_clamp_fusion.4), kind=kCustom, calls=%fused_computation.1.clone.1 | custom fusion | bytes 31457600 | tf_op jit(solution)/shard_map/while/body/eval_jaxpr/jit(_take)/gather | solution.py:74
  177.3 8.0 %fusion.30 = f32[8,3,2,16,256]{4,3,2,1,0:T(8,128)S(1)} fusion(bf16[8,10,3,128,256]{4,3,2,1,0:T(8,128)(2,1)} %bitcast.98, pred[8,10]{1,0:T(8,128)(4,1)S(1)} %copy-done.5, bf16[8,10,3,2,16,128]{5,4,3,2,1,0:T(8,128)(2,1)} %bitcast.99, pred[8,10]{1,0:T(8,128)(4,1)S(1)} %copy-done.6, bf16[8,10]{1,0:T(8,128)(2,1)S(1)} %fusion.29), kind=kOutput, calls=%fused_computation.8.clone.1 | convolution fusion | flops 513146880 | bytes 18481472 | tf_op jit(solution)/shard_map/while/body/eval_jaxpr/fsarkt,frktc->rfsac/dot_general | solution.py:75
  200.1 8.2 %gather_fusion = bf16[80,3,128,256]{3,2,1,0:T(8,128)(2,1)} fusion(bf16[3,8,128,256]{3,2,1,0:T(8,128)(2,1)S(1)} %dynamic-slice_bitcast_fusion.2, s32[1024]{0:T(1024)S(1)} %pad_clamp_fusion.4), kind=kCustom, calls=%fused_computation.1.clone.1 | custom fusion | bytes 31457600 | tf_op jit(solution)/shard_map/while/body/eval_jaxpr/jit(_take)/gather | solution.py:74
  212.4 8.0 %fusion.30 = f32[8,3,2,16,256]{4,3,2,1,0:T(8,128)S(1)} fusion(bf16[8,10,3,128,256]{4,3,2,1,0:T(8,128)(2,1)} %bitcast.98, pred[8,10]{1,0:T(8,128)(4,1)S(1)} %copy-done.5, bf16[8,10,3,2,16,128]{5,4,3,2,1,0:T(8,128)(2,1)} %bitcast.99, pred[8,10]{1,0:T(8,128)(4,1)S(1)} %copy-done.6, bf16[8,10]{1,0:T(8,128)(2,1)S(1)} %fusion.29), kind=kOutput, calls=%fused_computation.8.clone.1 | convolution fusion | flops 513146880 | bytes 18481472 | tf_op jit(solution)/shard_map/while/body/eval_jaxpr/fsarkt,frktc->rfsac/dot_general | solution.py:75
  235.1 8.1 %gather_fusion = bf16[80,3,128,256]{3,2,1,0:T(8,128)(2,1)} fusion(bf16[3,8,128,256]{3,2,1,0:T(8,128)(2,1)S(1)} %dynamic-slice_bitcast_fusion.2, s32[1024]{0:T(1024)S(1)} %pad_clamp_fusion.4), kind=kCustom, calls=%fused_computation.1.clone.1 | custom fusion | bytes 31457600 | tf_op jit(solution)/shard_map/while/body/eval_jaxpr/jit(_take)/gather | solution.py:74
  247.5 8.0 %fusion.30 = f32[8,3,2,16,256]{4,3,2,1,0:T(8,128)S(1)} fusion(bf16[8,10,3,128,256]{4,3,2,1,0:T(8,128)(2,1)} %bitcast.98, pred[8,10]{1,0:T(8,128)(4,1)S(1)} %copy-done.5, bf16[8,10,3,2,16,128]{5,4,3,2,1,0:T(8,128)(2,1)} %bitcast.99, pred[8,10]{1,0:T(8,128)(4,1)S(1)} %copy-done.6, bf16[8,10]{1,0:T(8,128)(2,1)S(1)} %fusion.29), kind=kOutput, calls=%fused_computation.8.clone.1 | convolution fusion | flops 513146880 | bytes 18481472 | tf_op jit(solution)/shard_map/while/body/eval_jaxpr/fsarkt,frktc->rfsac/dot_general | solution.py:75
  257.3 6.7 %collective-permute-start = (bf16[3,2,16,1024]{3,2,1,0:T(8,128)(2,1)S(1)}, bf16[3,2,16,1024]{3,2,1,0:T(8,128)(2,1)S(1)}, u32[]{:S(2)}, u32[]{:S(2)}) collective-permute-start(bf16[3,2,16,1024]{3,2,1,0:T(8,128)(2,1)S(1)} %get-tuple-element.365), channel_id=1, source_target_pairs={{2,0},{4,2},{6,4},{8,6},{10,8},{12,10},{14,12},{16,14},{18,16},{20... | collective-permute-start | bytes 589832 | tf_op jit(solution)/shard_map/while/body/eval_jaxpr/ppermute | solution.py:19
  270.3 8.2 %gather_fusion = bf16[80,3,128,256]{3,2,1,0:T(8,128)(2,1)} fusion(bf16[3,8,128,256]{3,2,1,0:T(8,128)(2,1)S(1)} %dynamic-slice_bitcast_fusion.2, s32[1024]{0:T(1024)S(1)} %pad_clamp_fusion.4), kind=kCustom, calls=%fused_computation.1.clone.1 | custom fusion | bytes 31457600 | tf_op jit(solution)/shard_map/while/body/eval_jaxpr/jit(_take)/gather | solution.py:74
  282.7 8.0 %fusion.30 = f32[8,3,2,16,256]{4,3,2,1,0:T(8,128)S(1)} fusion(bf16[8,10,3,128,256]{4,3,2,1,0:T(8,128)(2,1)} %bitcast.98, pred[8,10]{1,0:T(8,128)(4,1)S(1)} %copy-done.5, bf16[8,10,3,2,16,128]{5,4,3,2,1,0:T(8,128)(2,1)} %bitcast.99, pred[8,10]{1,0:T(8,128)(4,1)S(1)} %copy-done.6, bf16[8,10]{1,0:T(8,128)(2,1)S(1)} %fusion.29), kind=kOutput, calls=%fused_computation.8.clone.1 | convolution fusion | flops 513146880 | bytes 18481472 | tf_op jit(solution)/shard_map/while/body/eval_jaxpr/fsarkt,frktc->rfsac/dot_general | solution.py:75
  305.4 8.1 %gather_fusion = bf16[80,3,128,256]{3,2,1,0:T(8,128)(2,1)} fusion(bf16[3,8,128,256]{3,2,1,0:T(8,128)(2,1)S(1)} %dynamic-slice_bitcast_fusion.2, s32[1024]{0:T(1024)S(1)} %pad_clamp_fusion.4), kind=kCustom, calls=%fused_computation.1.clone.1 | custom fusion | bytes 31457600 | tf_op jit(solution)/shard_map/while/body/eval_jaxpr/jit(_take)/gather | solution.py:74
  317.7 8.0 %fusion.30 = f32[8,3,2,16,256]{4,3,2,1,0:T(8,128)S(1)} fusion(bf16[8,10,3,128,256]{4,3,2,1,0:T(8,128)(2,1)} %bitcast.98, pred[8,10]{1,0:T(8,128)(4,1)S(1)} %copy-done.5, bf16[8,10,3,2,16,128]{5,4,3,2,1,0:T(8,128)(2,1)} %bitcast.99, pred[8,10]{1,0:T(8,128)(4,1)S(1)} %copy-done.6, bf16[8,10]{1,0:T(8,128)(2,1)S(1)} %fusion.29), kind=kOutput, calls=%fused_computation.8.clone.1 | convolution fusion | flops 513146880 | bytes 18481472 | tf_op jit(solution)/shard_map/while/body/eval_jaxpr/fsarkt,frktc->rfsac/dot_general | solution.py:75
  340.5 8.2 %gather_fusion = bf16[80,3,128,256]{3,2,1,0:T(8,128)(2,1)} fusion(bf16[3,8,128,256]{3,2,1,0:T(8,128)(2,1)S(1)} %dynamic-slice_bitcast_fusion.2, s32[1024]{0:T(1024)S(1)} %pad_clamp_fusion.4), kind=kCustom, calls=%fused_computation.1.clone.1 | custom fusion | bytes 31457600 | tf_op jit(solution)/shard_map/while/body/eval_jaxpr/jit(_take)/gather | solution.py:74
  352.9 8.0 %fusion.30 = f32[8,3,2,16,256]{4,3,2,1,0:T(8,128)S(1)} fusion(bf16[8,10,3,128,256]{4,3,2,1,0:T(8,128)(2,1)} %bitcast.98, pred[8,10]{1,0:T(8,128)(4,1)S(1)} %copy-done.5, bf16[8,10,3,2,16,128]{5,4,3,2,1,0:T(8,128)(2,1)} %bitcast.99, pred[8,10]{1,0:T(8,128)(4,1)S(1)} %copy-done.6, bf16[8,10]{1,0:T(8,128)(2,1)S(1)} %fusion.29), kind=kOutput, calls=%fused_computation.8.clone.1 | convolution fusion | flops 513146880 | bytes 18481472 | tf_op jit(solution)/shard_map/while/body/eval_jaxpr/fsarkt,frktc->rfsac/dot_general | solution.py:75
  375.6 8.2 %gather_fusion = bf16[80,3,128,256]{3,2,1,0:T(8,128)(2,1)} fusion(bf16[3,8,128,256]{3,2,1,0:T(8,128)(2,1)S(1)} %dynamic-slice_bitcast_fusion.2, s32[1024]{0:T(1024)S(1)} %pad_clamp_fusion.4), kind=kCustom, calls=%fused_computation.1.clone.1 | custom fusion | bytes 31457600 | tf_op jit(solution)/shard_map/while/body/eval_jaxpr/jit(_take)/gather | solution.py:74
  387.9 8.0 %fusion.30 = f32[8,3,2,16,256]{4,3,2,1,0:T(8,128)S(1)} fusion(bf16[8,10,3,128,256]{4,3,2,1,0:T(8,128)(2,1)} %bitcast.98, pred[8,10]{1,0:T(8,128)(4,1)S(1)} %copy-done.5, bf16[8,10,3,2,16,128]{5,4,3,2,1,0:T(8,128)(2,1)} %bitcast.99, pred[8,10]{1,0:T(8,128)(4,1)S(1)} %copy-done.6, bf16[8,10]{1,0:T(8,128)(2,1)S(1)} %fusion.29), kind=kOutput, calls=%fused_computation.8.clone.1 | convolution fusion | flops 513146880 | bytes 18481472 | tf_op jit(solution)/shard_map/while/body/eval_jaxpr/fsarkt,frktc->rfsac/dot_general | solution.py:75
  410.7 8.2 %gather_fusion = bf16[80,3,128,256]{3,2,1,0:T(8,128)(2,1)} fusion(bf16[3,8,128,256]{3,2,1,0:T(8,128)(2,1)S(1)} %dynamic-slice_bitcast_fusion.2, s32[1024]{0:T(1024)S(1)} %pad_clamp_fusion.4), kind=kCustom, calls=%fused_computation.1.clone.1 | custom fusion | bytes 31457600 | tf_op jit(solution)/shard_map/while/body/eval_jaxpr/jit(_take)/gather | solution.py:74
  423.0 8.0 %fusion.30 = f32[8,3,2,16,256]{4,3,2,1,0:T(8,128)S(1)} fusion(bf16[8,10,3,128,256]{4,3,2,1,0:T(8,128)(2,1)} %bitcast.98, pred[8,10]{1,0:T(8,128)(4,1)S(1)} %copy-done.5, bf16[8,10,3,2,16,128]{5,4,3,2,1,0:T(8,128)(2,1)} %bitcast.99, pred[8,10]{1,0:T(8,128)(4,1)S(1)} %copy-done.6, bf16[8,10]{1,0:T(8,128)(2,1)S(1)} %fusion.29), kind=kOutput, calls=%fused_computation.8.clone.1 | convolution fusion | flops 513146880 | bytes 18481472 | tf_op jit(solution)/shard_map/while/body/eval_jaxpr/fsarkt,frktc->rfsac/dot_general | solution.py:75
  433.6 10.9 %all_to_all.10 = f32[8,1,1024]{2,1,0:T(1,128)S(1)} all-to-all(f32[8,1,1024]{2,1,0:T(1,128)S(1)} %reshape.218), channel_id=1, replica_groups=mesh['depth'=8,'lat'=32,'freq'=2] {'depth'}, dimensions={0} | all-to-all | bytes 65536 | tf_op jit(solution)/shard_map/all_to_all | solution.py:58
  444.5 8.4 %psum.7 = f32[1024]{0:T(1024)S(1)} all-reduce(f32[1024]{0:T(1024)S(1)} %reduce_sum.20), channel_id=1, replica_groups=mesh['depth'=8,'lat'=32,'freq'=2] {'freq'}, use_global_device_ids=true, to_apply=%region_4.5 | all-reduce | flops 1024 | bytes 8192 | tf_op jit(solution)/shard_map/psum | solution.py:119
  (271 shorter events, 143.4 us)
Async XLA Ops:
  6.5 32.0 %copy-start = (bf16[3,2,128,1024]{3,2,1,0:T(8,128)(2,1)S(1)}, bf16[3,2,128,1024]{3,2,1,0:T(8,128)(2,1)}, u32[]{:S(2)}) copy-start(bf16[3,2,128,1024]{3,2,1,0:T(8,128)(2,1)} %param.8) | copy-start | bytes 4718596
  6.5 144.3 %all-gather.2.cloned.1.call-start = ((), (), s32[]{:S(2)}) async-start(), calls=%async_computation.2 | async-start | bytes 14155776 | tf_op jit(solution)/shard_map/all_gather | solution.py:97
  8.6 30.8 %all-to-all-start = ((f32[8,1,1024]{2,1,0:T(1,128)}), f32[8,1,1024]{2,1,0:T(1,128)S(1)}, u32[]{:S(2)}, u32[]{:S(2)}) async-start(f32[8,1,1024]{2,1,0:T(1,128)} %broadcast_in_dim.88), calls=%async_computation | async-start | bytes 65536 | tf_op jit(solution)/shard_map/all_to_all | solution.py:37
  150.9 10.4 %copy-start.1 = (s32[8,8,10]{2,1,0:T(8,128)}, s32[8,8,10]{2,1,0:T(8,128)S(1)}, u32[]{:S(2)}) copy-start(s32[8,8,10]{2,1,0:T(8,128)S(1)} %get-tuple-element.381) | copy-start | bytes 7684 | tf_op jit(solution)/shard_map/while
  150.9 10.4 %copy-start.3 = (s32[8,8,10]{2,1,0:T(8,128)}, s32[8,8,10]{2,1,0:T(8,128)S(1)}, u32[]{:S(2)}) copy-start(s32[8,8,10]{2,1,0:T(8,128)S(1)} %get-tuple-element.378) | copy-start | bytes 7684 | tf_op jit(solution)/shard_map/while
  150.9 22.9 %collective-permute-start = (bf16[3,2,16,1024]{3,2,1,0:T(8,128)(2,1)S(1)}, bf16[3,2,16,1024]{3,2,1,0:T(8,128)(2,1)S(1)}, u32[]{:S(2)}, u32[]{:S(2)}) collective-permute-start(bf16[3,2,16,1024]{3,2,1,0:T(8,128)(2,1)S(1)} %get-tuple-element.365), channel_id=1, source_target_pairs={{2,0},{4,2},{6,4},{8,6},{10,8},{12,10},{14,12},{16,14},{18,16},{20... | collective-permute-start | bytes 589832 | tf_op jit(solution)/shard_map/while/body/eval_jaxpr/ppermute | solution.py:19
  158.7 15.1 %collective-permute-start.1 = (bf16[3,2,16,1024]{3,2,1,0:T(8,128)(2,1)S(1)}, bf16[3,2,16,1024]{3,2,1,0:T(8,128)(2,1)}, u32[]{:S(2)}, u32[]{:S(2)}) collective-permute-start(bf16[3,2,16,1024]{3,2,1,0:T(8,128)(2,1)S(1)} %get-tuple-element.365), channel_id=1, source_target_pairs={{0,2},{2,4},{4,6},{6,8},{8,10},{10,12},{12,14},{14,16},{16,18},{18... | collective-permute-start | bytes 589832 | tf_op jit(solution)/shard_map/while/body/eval_jaxpr/ppermute | solution.py:16
  187.0 9.4 %copy-start.3 = (s32[8,8,10]{2,1,0:T(8,128)}, s32[8,8,10]{2,1,0:T(8,128)S(1)}, u32[]{:S(2)}) copy-start(s32[8,8,10]{2,1,0:T(8,128)S(1)} %get-tuple-element.378) | copy-start | bytes 7684 | tf_op jit(solution)/shard_map/while
  187.1 21.9 %collective-permute-start = (bf16[3,2,16,1024]{3,2,1,0:T(8,128)(2,1)S(1)}, bf16[3,2,16,1024]{3,2,1,0:T(8,128)(2,1)S(1)}, u32[]{:S(2)}, u32[]{:S(2)}) collective-permute-start(bf16[3,2,16,1024]{3,2,1,0:T(8,128)(2,1)S(1)} %get-tuple-element.365), channel_id=1, source_target_pairs={{2,0},{4,2},{6,4},{8,6},{10,8},{12,10},{14,12},{16,14},{18,16},{20... | collective-permute-start | bytes 589832 | tf_op jit(solution)/shard_map/while/body/eval_jaxpr/ppermute | solution.py:19
  193.8 15.2 %collective-permute-start.1 = (bf16[3,2,16,1024]{3,2,1,0:T(8,128)(2,1)S(1)}, bf16[3,2,16,1024]{3,2,1,0:T(8,128)(2,1)}, u32[]{:S(2)}, u32[]{:S(2)}) collective-permute-start(bf16[3,2,16,1024]{3,2,1,0:T(8,128)(2,1)S(1)} %get-tuple-element.365), channel_id=1, source_target_pairs={{0,2},{2,4},{4,6},{6,8},{8,10},{10,12},{12,14},{14,16},{16,18},{18... | collective-permute-start | bytes 589832 | tf_op jit(solution)/shard_map/while/body/eval_jaxpr/ppermute | solution.py:16
  222.2 21.8 %collective-permute-start = (bf16[3,2,16,1024]{3,2,1,0:T(8,128)(2,1)S(1)}, bf16[3,2,16,1024]{3,2,1,0:T(8,128)(2,1)S(1)}, u32[]{:S(2)}, u32[]{:S(2)}) collective-permute-start(bf16[3,2,16,1024]{3,2,1,0:T(8,128)(2,1)S(1)} %get-tuple-element.365), channel_id=1, source_target_pairs={{2,0},{4,2},{6,4},{8,6},{10,8},{12,10},{14,12},{16,14},{18,16},{20... | collective-permute-start | bytes 589832 | tf_op jit(solution)/shard_map/while/body/eval_jaxpr/ppermute | solution.py:19
  228.9 15.1 %collective-permute-start.1 = (bf16[3,2,16,1024]{3,2,1,0:T(8,128)(2,1)S(1)}, bf16[3,2,16,1024]{3,2,1,0:T(8,128)(2,1)}, u32[]{:S(2)}, u32[]{:S(2)}) collective-permute-start(bf16[3,2,16,1024]{3,2,1,0:T(8,128)(2,1)S(1)} %get-tuple-element.365), channel_id=1, source_target_pairs={{0,2},{2,4},{4,6},{6,8},{8,10},{10,12},{12,14},{14,16},{16,18},{18... | collective-permute-start | bytes 589832 | tf_op jit(solution)/shard_map/while/body/eval_jaxpr/ppermute | solution.py:16
  257.3 9.4 %copy-start.1 = (s32[8,8,10]{2,1,0:T(8,128)}, s32[8,8,10]{2,1,0:T(8,128)S(1)}, u32[]{:S(2)}) copy-start(s32[8,8,10]{2,1,0:T(8,128)S(1)} %get-tuple-element.381) | copy-start | bytes 7684 | tf_op jit(solution)/shard_map/while
  257.3 9.4 %copy-start.3 = (s32[8,8,10]{2,1,0:T(8,128)}, s32[8,8,10]{2,1,0:T(8,128)S(1)}, u32[]{:S(2)}) copy-start(s32[8,8,10]{2,1,0:T(8,128)S(1)} %get-tuple-element.378) | copy-start | bytes 7684 | tf_op jit(solution)/shard_map/while
  257.3 21.9 %collective-permute-start = (bf16[3,2,16,1024]{3,2,1,0:T(8,128)(2,1)S(1)}, bf16[3,2,16,1024]{3,2,1,0:T(8,128)(2,1)S(1)}, u32[]{:S(2)}, u32[]{:S(2)}) collective-permute-start(bf16[3,2,16,1024]{3,2,1,0:T(8,128)(2,1)S(1)} %get-tuple-element.365), channel_id=1, source_target_pairs={{2,0},{4,2},{6,4},{8,6},{10,8},{12,10},{14,12},{16,14},{18,16},{20... | collective-permute-start | bytes 589832 | tf_op jit(solution)/shard_map/while/body/eval_jaxpr/ppermute | solution.py:19
  264.0 15.2 %collective-permute-start.1 = (bf16[3,2,16,1024]{3,2,1,0:T(8,128)(2,1)S(1)}, bf16[3,2,16,1024]{3,2,1,0:T(8,128)(2,1)}, u32[]{:S(2)}, u32[]{:S(2)}) collective-permute-start(bf16[3,2,16,1024]{3,2,1,0:T(8,128)(2,1)S(1)} %get-tuple-element.365), channel_id=1, source_target_pairs={{0,2},{2,4},{4,6},{6,8},{8,10},{10,12},{12,14},{14,16},{16,18},{18... | collective-permute-start | bytes 589832 | tf_op jit(solution)/shard_map/while/body/eval_jaxpr/ppermute | solution.py:16
  292.4 21.8 %collective-permute-start = (bf16[3,2,16,1024]{3,2,1,0:T(8,128)(2,1)S(1)}, bf16[3,2,16,1024]{3,2,1,0:T(8,128)(2,1)S(1)}, u32[]{:S(2)}, u32[]{:S(2)}) collective-permute-start(bf16[3,2,16,1024]{3,2,1,0:T(8,128)(2,1)S(1)} %get-tuple-element.365), channel_id=1, source_target_pairs={{2,0},{4,2},{6,4},{8,6},{10,8},{12,10},{14,12},{16,14},{18,16},{20... | collective-permute-start | bytes 589832 | tf_op jit(solution)/shard_map/while/body/eval_jaxpr/ppermute | solution.py:19
  299.1 15.1 %collective-permute-start.1 = (bf16[3,2,16,1024]{3,2,1,0:T(8,128)(2,1)S(1)}, bf16[3,2,16,1024]{3,2,1,0:T(8,128)(2,1)}, u32[]{:S(2)}, u32[]{:S(2)}) collective-permute-start(bf16[3,2,16,1024]{3,2,1,0:T(8,128)(2,1)S(1)} %get-tuple-element.365), channel_id=1, source_target_pairs={{0,2},{2,4},{4,6},{6,8},{8,10},{10,12},{12,14},{14,16},{16,18},{18... | collective-permute-start | bytes 589832 | tf_op jit(solution)/shard_map/while/body/eval_jaxpr/ppermute | solution.py:16
  327.5 21.9 %collective-permute-start = (bf16[3,2,16,1024]{3,2,1,0:T(8,128)(2,1)S(1)}, bf16[3,2,16,1024]{3,2,1,0:T(8,128)(2,1)S(1)}, u32[]{:S(2)}, u32[]{:S(2)}) collective-permute-start(bf16[3,2,16,1024]{3,2,1,0:T(8,128)(2,1)S(1)} %get-tuple-element.365), channel_id=1, source_target_pairs={{2,0},{4,2},{6,4},{8,6},{10,8},{12,10},{14,12},{16,14},{18,16},{20... | collective-permute-start | bytes 589832 | tf_op jit(solution)/shard_map/while/body/eval_jaxpr/ppermute | solution.py:19
  334.2 15.2 %collective-permute-start.1 = (bf16[3,2,16,1024]{3,2,1,0:T(8,128)(2,1)S(1)}, bf16[3,2,16,1024]{3,2,1,0:T(8,128)(2,1)}, u32[]{:S(2)}, u32[]{:S(2)}) collective-permute-start(bf16[3,2,16,1024]{3,2,1,0:T(8,128)(2,1)S(1)} %get-tuple-element.365), channel_id=1, source_target_pairs={{0,2},{2,4},{4,6},{6,8},{8,10},{10,12},{12,14},{14,16},{16,18},{18... | collective-permute-start | bytes 589832 | tf_op jit(solution)/shard_map/while/body/eval_jaxpr/ppermute | solution.py:16
  362.7 21.8 %collective-permute-start = (bf16[3,2,16,1024]{3,2,1,0:T(8,128)(2,1)S(1)}, bf16[3,2,16,1024]{3,2,1,0:T(8,128)(2,1)S(1)}, u32[]{:S(2)}, u32[]{:S(2)}) collective-permute-start(bf16[3,2,16,1024]{3,2,1,0:T(8,128)(2,1)S(1)} %get-tuple-element.365), channel_id=1, source_target_pairs={{2,0},{4,2},{6,4},{8,6},{10,8},{12,10},{14,12},{16,14},{18,16},{20... | collective-permute-start | bytes 589832 | tf_op jit(solution)/shard_map/while/body/eval_jaxpr/ppermute | solution.py:19
  369.3 15.2 %collective-permute-start.1 = (bf16[3,2,16,1024]{3,2,1,0:T(8,128)(2,1)S(1)}, bf16[3,2,16,1024]{3,2,1,0:T(8,128)(2,1)}, u32[]{:S(2)}, u32[]{:S(2)}) collective-permute-start(bf16[3,2,16,1024]{3,2,1,0:T(8,128)(2,1)S(1)} %get-tuple-element.365), channel_id=1, source_target_pairs={{0,2},{2,4},{4,6},{6,8},{8,10},{10,12},{12,14},{14,16},{16,18},{18... | collective-permute-start | bytes 589832 | tf_op jit(solution)/shard_map/while/body/eval_jaxpr/ppermute | solution.py:16
  397.7 21.8 %collective-permute-start = (bf16[3,2,16,1024]{3,2,1,0:T(8,128)(2,1)S(1)}, bf16[3,2,16,1024]{3,2,1,0:T(8,128)(2,1)S(1)}, u32[]{:S(2)}, u32[]{:S(2)}) collective-permute-start(bf16[3,2,16,1024]{3,2,1,0:T(8,128)(2,1)S(1)} %get-tuple-element.365), channel_id=1, source_target_pairs={{2,0},{4,2},{6,4},{8,6},{10,8},{12,10},{14,12},{16,14},{18,16},{20... | collective-permute-start | bytes 589832 | tf_op jit(solution)/shard_map/while/body/eval_jaxpr/ppermute | solution.py:19
  404.4 15.1 %collective-permute-start.1 = (bf16[3,2,16,1024]{3,2,1,0:T(8,128)(2,1)S(1)}, bf16[3,2,16,1024]{3,2,1,0:T(8,128)(2,1)}, u32[]{:S(2)}, u32[]{:S(2)}) collective-permute-start(bf16[3,2,16,1024]{3,2,1,0:T(8,128)(2,1)S(1)} %get-tuple-element.365), channel_id=1, source_target_pairs={{0,2},{2,4},{4,6},{6,8},{8,10},{10,12},{12,14},{14,16},{16,18},{18... | collective-permute-start | bytes 589832 | tf_op jit(solution)/shard_map/while/body/eval_jaxpr/ppermute | solution.py:16
  (43 other events, 169.2 us)
Sparse Core Ops, SparseCore 0:
  9.4 141.3 all-gather.1
where the time goes:
time: 463 us; the launch traced here: 460 us
  local copies, waits for them, and re-layouts  114 us (25%)
  waiting for transfers between devices  112 us (24%)
  starting transfers between devices  77.6 us (17%)
  matrix products  64.4 us (14%)
  blocking collectives  40.1 us (9%)
  other arithmetic  38.8 us (8%)
  between operations  13.4 us (3%)
    all_gather x1, waiting for transfers between devices, per_device(): pool_all = lax.all_gather(pool, 'depth', axis=0, tiled=True)  111 us
    gather x8, local copies, waits for them, and re-layouts, extrapolate(): chosen = jnp.take(pool_level, block_level, axis=1)  65.3 us
    dot_general x8, matrix products, extrapolate(): jnp.einsum('fsarkt,frktc->rfsac', picked, chosen, preferred_element_type=...  64.4 us
    ppermute x8, starting transfers between devices, extended_2(): lax.ppermute(lax.slice_in_dim(block, 0, width, axis=dim), axis, backward)  54.6 us
    all_gather x1, blocking collectives, in_one_piece(): lax.all_gather(both, axis, axis=dim, tiled=True)  20.8 us
    gather x8, local copies, waits for them, and re-layouts, extrapolate(): jnp.take(tile_grid, local_ids, axis=3)  19.3 us
    ppermute x8, starting transfers between devices, extended_2(): lax.ppermute(lax.slice_in_dim(block, block.shape[dim] - width, None, axis...  15.4 us
    squeeze x8, local copies, waits for them, and re-layouts, level_step(): lax.dynamic_index_in_dim(pool_all, level_index, 0, keepdims=False)  12.1 us
  transfers between devices with their start and end apart: 18, of which 1 were waited for; matrix products, arithmetic and copies ran while one was open for 24% of the time, Pallas kernels for 0%

commit v1 on v0

--- a/solution.py
+++ b/solution.py
@@ -5,6 +5,13 @@
 
 TILE = 128
 TILE_DEV = 8
+
+
+def all_by_exchange(shard, axis, along):
+    peers = lax.axis_size(axis)
+    pieces = jnp.stack([shard for _ in range(peers)])
+    pieces = lax.all_to_all(pieces, axis, split_axis=0, concat_axis=0)
+    return jnp.concatenate(pieces, axis=along)
 
 
 def extended_2(block, sides, width):
@@ -94,7 +101,7 @@
     lateral_width = surface.shape[3]
     shot_rows = shot_total // lax.axis_size("depth")
     own_shots = lax.dynamic_slice_in_dim(surface, depth_index * shot_rows, shot_rows, 2)
-    pool_all = lax.all_gather(pool, "depth", axis=0, tiled=True)
+    pool_all = all_by_exchange(pool, "depth", 0)
     ids_all, blocks_all, counts_all = in_one_piece((tile_ids, block_ids, counts), "depth", 0, 2)
     refl_all = gather_directly(refl, "depth", 0)
     level_total = pool_all.shape[0]

time: 463 us -> 633 us (1.37)
  blocking collectives: 40.1 us -> 326 us
  waiting for transfers between devices: 112 us -> 0.04 us
  between operations: 13.4 us -> 0.05 us
    all_gather x1, blocking collectives: 20.8 us -> 286 us  [in_one_piece(): lax.all_gather(both, axis, axis=dim, tiled=True)]
    all_gather x1 -> x0, waiting for transfers between devices: 111 us -> none  [per_device(): pool_all = lax.all_gather(pool, 'depth', axis=0, tiled=True)]
    all_to_all x0 -> x1, blocking collectives: none -> 14.3 us  [copy_for_each(): return lax.all_to_all(copies, axis, split_axis=0, concat_axis=0, tiled=True)]
    another operation x0 -> x1, local copies, waits for them, and re-layouts: none -> 7.53 us  [all_by_exchange(): pieces = jnp.stack([shard for _ in range(peers)])]
  transfers between devices with their start and end apart: 18 -> 17, of which waited for: 1 -> 0; matrix products, arithmetic and copies ran while one was open for 24% -> 17% of each run, Pallas kernels for 0% -> 0%
where the time goes in v1:
time: 633 us; the launch traced here: 630 us
  blocking collectives  326 us (52%)
  local copies, waits for them, and re-layouts  120 us (19%)
  starting transfers between devices  80.5 us (13%)
  matrix products  64.4 us (10%)
  other arithmetic  38.1 us (6%)
    all_gather x1, blocking collectives, in_one_piece(): lax.all_gather(both, axis, axis=dim, tiled=True)  286 us
    gather x8, local copies, waits for them, and re-layouts, extrapolate(): chosen = jnp.take(pool_level, block_level, axis=1)  65.3 us
    dot_general x8, matrix products, extrapolate(): jnp.einsum('fsarkt,frktc->rfsac', picked, chosen, preferred_element_type=...  64.4 us
    ppermute x8, starting transfers between devices, extended_2(): lax.ppermute(lax.slice_in_dim(block, 0, width, axis=dim), axis, backward)  59.7 us
    gather x8, local copies, waits for them, and re-layouts, extrapolate(): jnp.take(tile_grid, local_ids, axis=3)  19.3 us
    ppermute x8, starting transfers between devices, extended_2(): lax.ppermute(lax.slice_in_dim(block, block.shape[dim] - width, None, axis...  15.4 us
    all_to_all x1, blocking collectives, copy_for_each(): return lax.all_to_all(copies, axis, split_axis=0, concat_axis=0, tiled=True)  14.3 us
    psum x1, blocking collectives, per_device(): summed = lax.psum(image_local, 'freq')  14.2 us
  transfers between devices with their start and end apart: 17, of which 0 were waited for; matrix products, arithmetic and copies ran while one was open for 17% of the time, Pallas kernels for 0%

profile of v1, /device:TPU:1, one launch (start us, length us, event | category | flops | bytes accessed | tf_op | source)
XLA Modules:
  0.0 629.9 jit_solution(18368570831199511457)
XLA Ops:
  0.8 14.3 %all_to_all.15 = f32[8,1,1024]{2,1,0:T(1,128)S(1)} all-to-all(f32[8,1,1024]{2,1,0:T(1,128)S(1)} %broadcast_in_dim.88), channel_id=1, replica_groups=mesh['depth'=8,'lat'=32,'freq'=2] {'depth'}, dimensions={0} | all-to-all | bytes 65536 | tf_op jit(solution)/shard_map/all_to_all | solution.py:44
  15.2 7.5 %stack.27 = bf16[8,1,3,8,128,256]{5,4,3,2,1,0:T(8,128)(2,1)} broadcast(bf16[3,8,128,256]{3,2,1,0:T(8,128)(2,1)} %bitcast.102), dimensions={2,3,4,5} | broadcast | bytes 14155776 | tf_op jit(solution)/shard_map/stack | solution.py:12
  28.3 285.6 %all_gather.3 = s32[8,8,21]{2,1,0:T(8,128)S(1)} all-gather(s32[1,8,21]{2,1,0:T(8,128)S(1)} %pad_add_fusion), channel_id=1, replica_groups=mesh['depth'=8,'lat'=32,'freq'=2] {'depth'}, dimensions={0}, use_global_device_ids=true | all-gather | bytes 6048 | tf_op jit(solution)/shard_map/all_gather | solution.py:34
  315.5 287.0 %while.17 = (s32[]{:T(128)}, bf16[3,2,16,1024]{3,2,1,0:T(8,128)(2,1)S(1)}, f32[8,1024]{1,0:T(8,128)}, s32[8,8,10]{2,1,0:T(8,128)S(1)}, s32[]{:T(128)}, /*index=5...) while((s32[]{:T(128)}, ...), condition=%wide.region_2.3_spmd, body=%wide.region_0.2_spmd.sunk | while | flops 515904960 | bytes 62015692 | solution.py:124
  315.5 12.9 %collective-permute-start = (bf16[3,2,16,1024]{3,2,1,0:T(8,128)(2,1)S(1)}, bf16[3,2,16,1024]{3,2,1,0:T(8,128)(2,1)S(1)}, u32[]{:S(2)}, u32[]{:S(2)}) collective-permute-start(bf16[3,2,16,1024]{3,2,1,0:T(8,128)(2,1)S(1)} %get-tuple-element.365), channel_id=1, source_target_pairs={{2,0},{4,2},{6,4},{8,6},{10,8},{12,10},{14,12},{16,14},{18,16},{20... | collective-permute-start | bytes 589832 | tf_op jit(solution)/shard_map/while/body/eval_jaxpr/ppermute | solution.py:26
  334.7 8.1 %gather_fusion = bf16[80,3,128,256]{3,2,1,0:T(8,128)(2,1)} fusion(bf16[3,8,128,256]{3,2,1,0:T(8,128)(2,1)S(1)} %dynamic-slice_bitcast_fusion.2, s32[1024]{0:T(1024)S(1)} %pad_clamp_fusion.4), kind=kCustom, calls=%fused_computation.1.clone.1 | custom fusion | bytes 31457600 | tf_op jit(solution)/shard_map/while/body/eval_jaxpr/jit(_take)/gather | solution.py:81
  347.0 8.0 %fusion.30 = f32[8,3,2,16,256]{4,3,2,1,0:T(8,128)S(1)} fusion(bf16[8,10,3,128,256]{4,3,2,1,0:T(8,128)(2,1)} %bitcast.100, pred[8,10]{1,0:T(8,128)(4,1)S(1)} %copy-done.5, bf16[8,10,3,2,16,128]{5,4,3,2,1,0:T(8,128)(2,1)} %bitcast.101, pred[8,10]{1,0:T(8,128)(4,1)S(1)} %copy-done.6, bf16[8,10]{1,0:T(8,128)(2,1)S(1)} %fusion.29), kind=kOutput, calls=%fused_computation.8.clone.1 | convolution fusion | flops 513146880 | bytes 18481472 | tf_op jit(solution)/shard_map/while/body/eval_jaxpr/fsarkt,frktc->rfsac/dot_general | solution.py:82
  369.8 8.2 %gather_fusion = bf16[80,3,128,256]{3,2,1,0:T(8,128)(2,1)} fusion(bf16[3,8,128,256]{3,2,1,0:T(8,128)(2,1)S(1)} %dynamic-slice_bitcast_fusion.2, s32[1024]{0:T(1024)S(1)} %pad_clamp_fusion.4), kind=kCustom, calls=%fused_computation.1.clone.1 | custom fusion | bytes 31457600 | tf_op jit(solution)/shard_map/while/body/eval_jaxpr/jit(_take)/gather | solution.py:81
  382.1 8.0 %fusion.30 = f32[8,3,2,16,256]{4,3,2,1,0:T(8,128)S(1)} fusion(bf16[8,10,3,128,256]{4,3,2,1,0:T(8,128)(2,1)} %bitcast.100, pred[8,10]{1,0:T(8,128)(4,1)S(1)} %copy-done.5, bf16[8,10,3,2,16,128]{5,4,3,2,1,0:T(8,128)(2,1)} %bitcast.101, pred[8,10]{1,0:T(8,128)(4,1)S(1)} %copy-done.6, bf16[8,10]{1,0:T(8,128)(2,1)S(1)} %fusion.29), kind=kOutput, calls=%fused_computation.8.clone.1 | convolution fusion | flops 513146880 | bytes 18481472 | tf_op jit(solution)/shard_map/while/body/eval_jaxpr/fsarkt,frktc->rfsac/dot_general | solution.py:82
  404.9 8.1 %gather_fusion = bf16[80,3,128,256]{3,2,1,0:T(8,128)(2,1)} fusion(bf16[3,8,128,256]{3,2,1,0:T(8,128)(2,1)S(1)} %dynamic-slice_bitcast_fusion.2, s32[1024]{0:T(1024)S(1)} %pad_clamp_fusion.4), kind=kCustom, calls=%fused_computation.1.clone.1 | custom fusion | bytes 31457600 | tf_op jit(solution)/shard_map/while/body/eval_jaxpr/jit(_take)/gather | solution.py:81
  417.2 8.0 %fusion.30 = f32[8,3,2,16,256]{4,3,2,1,0:T(8,128)S(1)} fusion(bf16[8,10,3,128,256]{4,3,2,1,0:T(8,128)(2,1)} %bitcast.100, pred[8,10]{1,0:T(8,128)(4,1)S(1)} %copy-done.5, bf16[8,10,3,2,16,128]{5,4,3,2,1,0:T(8,128)(2,1)} %bitcast.101, pred[8,10]{1,0:T(8,128)(4,1)S(1)} %copy-done.6, bf16[8,10]{1,0:T(8,128)(2,1)S(1)} %fusion.29), kind=kOutput, calls=%fused_computation.8.clone.1 | convolution fusion | flops 513146880 | bytes 18481472 | tf_op jit(solution)/shard_map/while/body/eval_jaxpr/fsarkt,frktc->rfsac/dot_general | solution.py:82
  427.0 6.7 %collective-permute-start = (bf16[3,2,16,1024]{3,2,1,0:T(8,128)(2,1)S(1)}, bf16[3,2,16,1024]{3,2,1,0:T(8,128)(2,1)S(1)}, u32[]{:S(2)}, u32[]{:S(2)}) collective-permute-start(bf16[3,2,16,1024]{3,2,1,0:T(8,128)(2,1)S(1)} %get-tuple-element.365), channel_id=1, source_target_pairs={{2,0},{4,2},{6,4},{8,6},{10,8},{12,10},{14,12},{16,14},{18,16},{20... | collective-permute-start | bytes 589832 | tf_op jit(solution)/shard_map/while/body/eval_jaxpr/ppermute | solution.py:26
  440.0 8.2 %gather_fusion = bf16[80,3,128,256]{3,2,1,0:T(8,128)(2,1)} fusion(bf16[3,8,128,256]{3,2,1,0:T(8,128)(2,1)S(1)} %dynamic-slice_bitcast_fusion.2, s32[1024]{0:T(1024)S(1)} %pad_clamp_fusion.4), kind=kCustom, calls=%fused_computation.1.clone.1 | custom fusion | bytes 31457600 | tf_op jit(solution)/shard_map/while/body/eval_jaxpr/jit(_take)/gather | solution.py:81
  452.4 8.0 %fusion.30 = f32[8,3,2,16,256]{4,3,2,1,0:T(8,128)S(1)} fusion(bf16[8,10,3,128,256]{4,3,2,1,0:T(8,128)(2,1)} %bitcast.100, pred[8,10]{1,0:T(8,128)(4,1)S(1)} %copy-done.5, bf16[8,10,3,2,16,128]{5,4,3,2,1,0:T(8,128)(2,1)} %bitcast.101, pred[8,10]{1,0:T(8,128)(4,1)S(1)} %copy-done.6, bf16[8,10]{1,0:T(8,128)(2,1)S(1)} %fusion.29), kind=kOutput, calls=%fused_computation.8.clone.1 | convolution fusion | flops 513146880 | bytes 18481472 | tf_op jit(solution)/shard_map/while/body/eval_jaxpr/fsarkt,frktc->rfsac/dot_general | solution.py:82
  475.1 8.1 %gather_fusion = bf16[80,3,128,256]{3,2,1,0:T(8,128)(2,1)} fusion(bf16[3,8,128,256]{3,2,1,0:T(8,128)(2,1)S(1)} %dynamic-slice_bitcast_fusion.2, s32[1024]{0:T(1024)S(1)} %pad_clamp_fusion.4), kind=kCustom, calls=%fused_computation.1.clone.1 | custom fusion | bytes 31457600 | tf_op jit(solution)/shard_map/while/body/eval_jaxpr/jit(_take)/gather | solution.py:81
  487.5 8.0 %fusion.30 = f32[8,3,2,16,256]{4,3,2,1,0:T(8,128)S(1)} fusion(bf16[8,10,3,128,256]{4,3,2,1,0:T(8,128)(2,1)} %bitcast.100, pred[8,10]{1,0:T(8,128)(4,1)S(1)} %copy-done.5, bf16[8,10,3,2,16,128]{5,4,3,2,1,0:T(8,128)(2,1)} %bitcast.101, pred[8,10]{1,0:T(8,128)(4,1)S(1)} %copy-done.6, bf16[8,10]{1,0:T(8,128)(2,1)S(1)} %fusion.29), kind=kOutput, calls=%fused_computation.8.clone.1 | convolution fusion | flops 513146880 | bytes 18481472 | tf_op jit(solution)/shard_map/while/body/eval_jaxpr/fsarkt,frktc->rfsac/dot_general | solution.py:82
  510.3 8.2 %gather_fusion = bf16[80,3,128,256]{3,2,1,0:T(8,128)(2,1)} fusion(bf16[3,8,128,256]{3,2,1,0:T(8,128)(2,1)S(1)} %dynamic-slice_bitcast_fusion.2, s32[1024]{0:T(1024)S(1)} %pad_clamp_fusion.4), kind=kCustom, calls=%fused_computation.1.clone.1 | custom fusion | bytes 31457600 | tf_op jit(solution)/shard_map/while/body/eval_jaxpr/jit(_take)/gather | solution.py:81
  522.6 8.0 %fusion.30 = f32[8,3,2,16,256]{4,3,2,1,0:T(8,128)S(1)} fusion(bf16[8,10,3,128,256]{4,3,2,1,0:T(8,128)(2,1)} %bitcast.100, pred[8,10]{1,0:T(8,128)(4,1)S(1)} %copy-done.5, bf16[8,10,3,2,16,128]{5,4,3,2,1,0:T(8,128)(2,1)} %bitcast.101, pred[8,10]{1,0:T(8,128)(4,1)S(1)} %copy-done.6, bf16[8,10]{1,0:T(8,128)(2,1)S(1)} %fusion.29), kind=kOutput, calls=%fused_computation.8.clone.1 | convolution fusion | flops 513146880 | bytes 18481472 | tf_op jit(solution)/shard_map/while/body/eval_jaxpr/fsarkt,frktc->rfsac/dot_general | solution.py:82
  545.3 8.2 %gather_fusion = bf16[80,3,128,256]{3,2,1,0:T(8,128)(2,1)} fusion(bf16[3,8,128,256]{3,2,1,0:T(8,128)(2,1)S(1)} %dynamic-slice_bitcast_fusion.2, s32[1024]{0:T(1024)S(1)} %pad_clamp_fusion.4), kind=kCustom, calls=%fused_computation.1.clone.1 | custom fusion | bytes 31457600 | tf_op jit(solution)/shard_map/while/body/eval_jaxpr/jit(_take)/gather | solution.py:81
  557.7 8.0 %fusion.30 = f32[8,3,2,16,256]{4,3,2,1,0:T(8,128)S(1)} fusion(bf16[8,10,3,128,256]{4,3,2,1,0:T(8,128)(2,1)} %bitcast.100, pred[8,10]{1,0:T(8,128)(4,1)S(1)} %copy-done.5, bf16[8,10,3,2,16,128]{5,4,3,2,1,0:T(8,128)(2,1)} %bitcast.101, pred[8,10]{1,0:T(8,128)(4,1)S(1)} %copy-done.6, bf16[8,10]{1,0:T(8,128)(2,1)S(1)} %fusion.29), kind=kOutput, calls=%fused_computation.8.clone.1 | convolution fusion | flops 513146880 | bytes 18481472 | tf_op jit(solution)/shard_map/while/body/eval_jaxpr/fsarkt,frktc->rfsac/dot_general | solution.py:82
  580.4 8.2 %gather_fusion = bf16[80,3,128,256]{3,2,1,0:T(8,128)(2,1)} fusion(bf16[3,8,128,256]{3,2,1,0:T(8,128)(2,1)S(1)} %dynamic-slice_bitcast_fusion.2, s32[1024]{0:T(1024)S(1)} %pad_clamp_fusion.4), kind=kCustom, calls=%fused_computation.1.clone.1 | custom fusion | bytes 31457600 | tf_op jit(solution)/shard_map/while/body/eval_jaxpr/jit(_take)/gather | solution.py:81
  592.8 8.0 %fusion.30 = f32[8,3,2,16,256]{4,3,2,1,0:T(8,128)S(1)} fusion(bf16[8,10,3,128,256]{4,3,2,1,0:T(8,128)(2,1)} %bitcast.100, pred[8,10]{1,0:T(8,128)(4,1)S(1)} %copy-done.5, bf16[8,10,3,2,16,128]{5,4,3,2,1,0:T(8,128)(2,1)} %bitcast.101, pred[8,10]{1,0:T(8,128)(4,1)S(1)} %copy-done.6, bf16[8,10]{1,0:T(8,128)(2,1)S(1)} %fusion.29), kind=kOutput, calls=%fused_computation.8.clone.1 | convolution fusion | flops 513146880 | bytes 18481472 | tf_op jit(solution)/shard_map/while/body/eval_jaxpr/fsarkt,frktc->rfsac/dot_general | solution.py:82
  603.3 11.7 %all_to_all.16 = f32[8,1,1024]{2,1,0:T(1,128)S(1)} all-to-all(f32[8,1,1024]{2,1,0:T(1,128)S(1)} %reshape.225), channel_id=1, replica_groups=mesh['depth'=8,'lat'=32,'freq'=2] {'depth'}, dimensions={0} | all-to-all | bytes 65536 | tf_op jit(solution)/shard_map/all_to_all | solution.py:65
  615.1 14.2 %psum.7 = f32[1024]{0:T(1024)S(1)} all-reduce(f32[1024]{0:T(1024)S(1)} %reduce_sum.20), channel_id=1, replica_groups=mesh['depth'=8,'lat'=32,'freq'=2] {'freq'}, use_global_device_ids=true, to_apply=%region_4.5 | all-reduce | flops 1024 | bytes 8192 | tf_op jit(solution)/shard_map/psum | solution.py:126
  (276 shorter events, 146.3 us)
Async XLA Ops:
  0.0 314.8 %copy-start = (bf16[3,2,128,1024]{3,2,1,0:T(8,128)(2,1)S(1)}, bf16[3,2,128,1024]{3,2,1,0:T(8,128)(2,1)}, u32[]{:S(2)}) copy-start(bf16[3,2,128,1024]{3,2,1,0:T(8,128)(2,1)} %param.8) | copy-start | bytes 4718596
  22.7 292.8 %all-to-all-start = ((bf16[8,1,3,8,128,256]{5,4,3,2,1,0:T(8,128)(2,1)}), bf16[8,1,3,8,128,256]{5,4,3,2,1,0:T(8,128)(2,1)}, u32[]{:S(2)}, u32[]{:S(2)}) async-start(bf16[8,1,3,8,128,256]{5,4,3,2,1,0:T(8,128)(2,1)} %stack.27), calls=%async_computation | async-start | bytes 25165824 | tf_op jit(solution)/shard_map/all_to_all | solution.py:13
  315.5 15.6 %copy-start.1 = (s32[8,8,10]{2,1,0:T(8,128)}, s32[8,8,10]{2,1,0:T(8,128)S(1)}, u32[]{:S(2)}) copy-start(s32[8,8,10]{2,1,0:T(8,128)S(1)} %get-tuple-element.381) | copy-start | bytes 7684 | tf_op jit(solution)/shard_map/while
  315.5 15.6 %copy-start.3 = (s32[8,8,10]{2,1,0:T(8,128)}, s32[8,8,10]{2,1,0:T(8,128)S(1)}, u32[]{:S(2)}) copy-start(s32[8,8,10]{2,1,0:T(8,128)S(1)} %get-tuple-element.378) | copy-start | bytes 7684 | tf_op jit(solution)/shard_map/while
  315.5 28.0 %collective-permute-start = (bf16[3,2,16,1024]{3,2,1,0:T(8,128)(2,1)S(1)}, bf16[3,2,16,1024]{3,2,1,0:T(8,128)(2,1)S(1)}, u32[]{:S(2)}, u32[]{:S(2)}) collective-permute-start(bf16[3,2,16,1024]{3,2,1,0:T(8,128)(2,1)S(1)} %get-tuple-element.365), channel_id=1, source_target_pairs={{2,0},{4,2},{6,4},{8,6},{10,8},{12,10},{14,12},{16,14},{18,16},{20... | collective-permute-start | bytes 589832 | tf_op jit(solution)/shard_map/while/body/eval_jaxpr/ppermute | solution.py:26
  328.4 15.1 %collective-permute-start.1 = (bf16[3,2,16,1024]{3,2,1,0:T(8,128)(2,1)S(1)}, bf16[3,2,16,1024]{3,2,1,0:T(8,128)(2,1)}, u32[]{:S(2)}, u32[]{:S(2)}) collective-permute-start(bf16[3,2,16,1024]{3,2,1,0:T(8,128)(2,1)S(1)} %get-tuple-element.365), channel_id=1, source_target_pairs={{0,2},{2,4},{4,6},{6,8},{8,10},{10,12},{12,14},{14,16},{16,18},{18... | collective-permute-start | bytes 589832 | tf_op jit(solution)/shard_map/while/body/eval_jaxpr/ppermute | solution.py:23
  356.8 9.4 %copy-start.3 = (s32[8,8,10]{2,1,0:T(8,128)}, s32[8,8,10]{2,1,0:T(8,128)S(1)}, u32[]{:S(2)}) copy-start(s32[8,8,10]{2,1,0:T(8,128)S(1)} %get-tuple-element.378) | copy-start | bytes 7684 | tf_op jit(solution)/shard_map/while
  356.8 21.9 %collective-permute-start = (bf16[3,2,16,1024]{3,2,1,0:T(8,128)(2,1)S(1)}, bf16[3,2,16,1024]{3,2,1,0:T(8,128)(2,1)S(1)}, u32[]{:S(2)}, u32[]{:S(2)}) collective-permute-start(bf16[3,2,16,1024]{3,2,1,0:T(8,128)(2,1)S(1)} %get-tuple-element.365), channel_id=1, source_target_pairs={{2,0},{4,2},{6,4},{8,6},{10,8},{12,10},{14,12},{16,14},{18,16},{20... | collective-permute-start | bytes 589832 | tf_op jit(solution)/shard_map/while/body/eval_jaxpr/ppermute | solution.py:26
  363.5 15.2 %collective-permute-start.1 = (bf16[3,2,16,1024]{3,2,1,0:T(8,128)(2,1)S(1)}, bf16[3,2,16,1024]{3,2,1,0:T(8,128)(2,1)}, u32[]{:S(2)}, u32[]{:S(2)}) collective-permute-start(bf16[3,2,16,1024]{3,2,1,0:T(8,128)(2,1)S(1)} %get-tuple-element.365), channel_id=1, source_target_pairs={{0,2},{2,4},{4,6},{6,8},{8,10},{10,12},{12,14},{14,16},{16,18},{18... | collective-permute-start | bytes 589832 | tf_op jit(solution)/shard_map/while/body/eval_jaxpr/ppermute | solution.py:23
  391.9 21.8 %collective-permute-start = (bf16[3,2,16,1024]{3,2,1,0:T(8,128)(2,1)S(1)}, bf16[3,2,16,1024]{3,2,1,0:T(8,128)(2,1)S(1)}, u32[]{:S(2)}, u32[]{:S(2)}) collective-permute-start(bf16[3,2,16,1024]{3,2,1,0:T(8,128)(2,1)S(1)} %get-tuple-element.365), channel_id=1, source_target_pairs={{2,0},{4,2},{6,4},{8,6},{10,8},{12,10},{14,12},{16,14},{18,16},{20... | collective-permute-start | bytes 589832 | tf_op jit(solution)/shard_map/while/body/eval_jaxpr/ppermute | solution.py:26
  398.6 15.1 %collective-permute-start.1 = (bf16[3,2,16,1024]{3,2,1,0:T(8,128)(2,1)S(1)}, bf16[3,2,16,1024]{3,2,1,0:T(8,128)(2,1)}, u32[]{:S(2)}, u32[]{:S(2)}) collective-permute-start(bf16[3,2,16,1024]{3,2,1,0:T(8,128)(2,1)S(1)} %get-tuple-element.365), channel_id=1, source_target_pairs={{0,2},{2,4},{4,6},{6,8},{8,10},{10,12},{12,14},{14,16},{16,18},{18... | collective-permute-start | bytes 589832 | tf_op jit(solution)/shard_map/while/body/eval_jaxpr/ppermute | solution.py:23
  427.0 9.4 %copy-start.1 = (s32[8,8,10]{2,1,0:T(8,128)}, s32[8,8,10]{2,1,0:T(8,128)S(1)}, u32[]{:S(2)}) copy-start(s32[8,8,10]{2,1,0:T(8,128)S(1)} %get-tuple-element.381) | copy-start | bytes 7684 | tf_op jit(solution)/shard_map/while
  427.0 9.4 %copy-start.3 = (s32[8,8,10]{2,1,0:T(8,128)}, s32[8,8,10]{2,1,0:T(8,128)S(1)}, u32[]{:S(2)}) copy-start(s32[8,8,10]{2,1,0:T(8,128)S(1)} %get-tuple-element.378) | copy-start | bytes 7684 | tf_op jit(solution)/shard_map/while
  427.0 21.9 %collective-permute-start = (bf16[3,2,16,1024]{3,2,1,0:T(8,128)(2,1)S(1)}, bf16[3,2,16,1024]{3,2,1,0:T(8,128)(2,1)S(1)}, u32[]{:S(2)}, u32[]{:S(2)}) collective-permute-start(bf16[3,2,16,1024]{3,2,1,0:T(8,128)(2,1)S(1)} %get-tuple-element.365), channel_id=1, source_target_pairs={{2,0},{4,2},{6,4},{8,6},{10,8},{12,10},{14,12},{16,14},{18,16},{20... | collective-permute-start | bytes 589832 | tf_op jit(solution)/shard_map/while/body/eval_jaxpr/ppermute | solution.py:26
  433.7 15.2 %collective-permute-start.1 = (bf16[3,2,16,1024]{3,2,1,0:T(8,128)(2,1)S(1)}, bf16[3,2,16,1024]{3,2,1,0:T(8,128)(2,1)}, u32[]{:S(2)}, u32[]{:S(2)}) collective-permute-start(bf16[3,2,16,1024]{3,2,1,0:T(8,128)(2,1)S(1)} %get-tuple-element.365), channel_id=1, source_target_pairs={{0,2},{2,4},{4,6},{6,8},{8,10},{10,12},{12,14},{14,16},{16,18},{18... | collective-permute-start | bytes 589832 | tf_op jit(solution)/shard_map/while/body/eval_jaxpr/ppermute | solution.py:23
  462.2 21.8 %collective-permute-start = (bf16[3,2,16,1024]{3,2,1,0:T(8,128)(2,1)S(1)}, bf16[3,2,16,1024]{3,2,1,0:T(8,128)(2,1)S(1)}, u32[]{:S(2)}, u32[]{:S(2)}) collective-permute-start(bf16[3,2,16,1024]{3,2,1,0:T(8,128)(2,1)S(1)} %get-tuple-element.365), channel_id=1, source_target_pairs={{2,0},{4,2},{6,4},{8,6},{10,8},{12,10},{14,12},{16,14},{18,16},{20... | collective-permute-start | bytes 589832 | tf_op jit(solution)/shard_map/while/body/eval_jaxpr/ppermute | solution.py:26
  468.9 15.1 %collective-permute-start.1 = (bf16[3,2,16,1024]{3,2,1,0:T(8,128)(2,1)S(1)}, bf16[3,2,16,1024]{3,2,1,0:T(8,128)(2,1)}, u32[]{:S(2)}, u32[]{:S(2)}) collective-permute-start(bf16[3,2,16,1024]{3,2,1,0:T(8,128)(2,1)S(1)} %get-tuple-element.365), channel_id=1, source_target_pairs={{0,2},{2,4},{4,6},{6,8},{8,10},{10,12},{12,14},{14,16},{16,18},{18... | collective-permute-start | bytes 589832 | tf_op jit(solution)/shard_map/while/body/eval_jaxpr/ppermute | solution.py:23
  497.2 9.4 %copy-start.3 = (s32[8,8,10]{2,1,0:T(8,128)}, s32[8,8,10]{2,1,0:T(8,128)S(1)}, u32[]{:S(2)}) copy-start(s32[8,8,10]{2,1,0:T(8,128)S(1)} %get-tuple-element.378) | copy-start | bytes 7684 | tf_op jit(solution)/shard_map/while
  497.2 21.9 %collective-permute-start = (bf16[3,2,16,1024]{3,2,1,0:T(8,128)(2,1)S(1)}, bf16[3,2,16,1024]{3,2,1,0:T(8,128)(2,1)S(1)}, u32[]{:S(2)}, u32[]{:S(2)}) collective-permute-start(bf16[3,2,16,1024]{3,2,1,0:T(8,128)(2,1)S(1)} %get-tuple-element.365), channel_id=1, source_target_pairs={{2,0},{4,2},{6,4},{8,6},{10,8},{12,10},{14,12},{16,14},{18,16},{20... | collective-permute-start | bytes 589832 | tf_op jit(solution)/shard_map/while/body/eval_jaxpr/ppermute | solution.py:26
  504.0 15.2 %collective-permute-start.1 = (bf16[3,2,16,1024]{3,2,1,0:T(8,128)(2,1)S(1)}, bf16[3,2,16,1024]{3,2,1,0:T(8,128)(2,1)}, u32[]{:S(2)}, u32[]{:S(2)}) collective-permute-start(bf16[3,2,16,1024]{3,2,1,0:T(8,128)(2,1)S(1)} %get-tuple-element.365), channel_id=1, source_target_pairs={{0,2},{2,4},{4,6},{6,8},{8,10},{10,12},{12,14},{14,16},{16,18},{18... | collective-permute-start | bytes 589832 | tf_op jit(solution)/shard_map/while/body/eval_jaxpr/ppermute | solution.py:23
  532.4 21.8 %collective-permute-start = (bf16[3,2,16,1024]{3,2,1,0:T(8,128)(2,1)S(1)}, bf16[3,2,16,1024]{3,2,1,0:T(8,128)(2,1)S(1)}, u32[]{:S(2)}, u32[]{:S(2)}) collective-permute-start(bf16[3,2,16,1024]{3,2,1,0:T(8,128)(2,1)S(1)} %get-tuple-element.365), channel_id=1, source_target_pairs={{2,0},{4,2},{6,4},{8,6},{10,8},{12,10},{14,12},{16,14},{18,16},{20... | collective-permute-start | bytes 589832 | tf_op jit(solution)/shard_map/while/body/eval_jaxpr/ppermute | solution.py:26
  539.0 15.2 %collective-permute-start.1 = (bf16[3,2,16,1024]{3,2,1,0:T(8,128)(2,1)S(1)}, bf16[3,2,16,1024]{3,2,1,0:T(8,128)(2,1)}, u32[]{:S(2)}, u32[]{:S(2)}) collective-permute-start(bf16[3,2,16,1024]{3,2,1,0:T(8,128)(2,1)S(1)} %get-tuple-element.365), channel_id=1, source_target_pairs={{0,2},{2,4},{4,6},{6,8},{8,10},{10,12},{12,14},{14,16},{16,18},{18... | collective-permute-start | bytes 589832 | tf_op jit(solution)/shard_map/while/body/eval_jaxpr/ppermute | solution.py:23
  567.4 21.8 %collective-permute-start = (bf16[3,2,16,1024]{3,2,1,0:T(8,128)(2,1)S(1)}, bf16[3,2,16,1024]{3,2,1,0:T(8,128)(2,1)S(1)}, u32[]{:S(2)}, u32[]{:S(2)}) collective-permute-start(bf16[3,2,16,1024]{3,2,1,0:T(8,128)(2,1)S(1)} %get-tuple-element.365), channel_id=1, source_target_pairs={{2,0},{4,2},{6,4},{8,6},{10,8},{12,10},{14,12},{16,14},{18,16},{20... | collective-permute-start | bytes 589832 | tf_op jit(solution)/shard_map/while/body/eval_jaxpr/ppermute | solution.py:26
  574.1 15.1 %collective-permute-start.1 = (bf16[3,2,16,1024]{3,2,1,0:T(8,128)(2,1)S(1)}, bf16[3,2,16,1024]{3,2,1,0:T(8,128)(2,1)}, u32[]{:S(2)}, u32[]{:S(2)}) collective-permute-start(bf16[3,2,16,1024]{3,2,1,0:T(8,128)(2,1)S(1)} %get-tuple-element.365), channel_id=1, source_target_pairs={{0,2},{2,4},{4,6},{6,8},{8,10},{10,12},{12,14},{14,16},{16,18},{18... | collective-permute-start | bytes 589832 | tf_op jit(solution)/shard_map/while/body/eval_jaxpr/ppermute | solution.py:23
  (45 other events, 176.5 us)
